TPU v7x, 32 devices: a whole 2x2x4 slice. The times are simulated.
32 devices in a mesh: band: 4 (over y, x), dom: 8 (over z, core).
Axes of the slice: x: 2, y: 2, z: 4, core: 2. Of those that a mesh axis runs over, the one named last changes fastest.
Arguments:
- wave: bfloat16 [48, 19, 13, 1024], P('dom', None, None, 'band'), parts along dimension 3, may hold values from -6 to 6
- kinetic: bfloat16 [343, 343], replicated, may hold values from -1 to 1, as said below
- cell_scale: float32 [48], P('dom'), may hold values from 0.5 to 2
- potential: float32 [48, 19, 13], P('dom'), may hold values from 0.2 to 2
- proj_values: bfloat16 [128, 343], P('dom'), may hold values from -0.23925781 to 0.23925781
- piece_cell: int32 [128], P('dom'), may hold values from 0 to 5
- piece_proj: int32 [128], P('dom'), may hold values from 0 to 255
- coupling: float32 [256], replicated, may hold values from 0.5 to 2
- center: float32 [1], replicated, may hold values from 9 to 11
- halfwidth: float32 [1], replicated, may hold values from 14 to 18
Outputs:
- filtered: float32 [48, 19, 13, 1024], P('dom', None, None, 'band'), parts along dimension 3
There are 4 independent parts, one for each index of `band`. A program takes and returns all parts, laid end to end along the dimension named above; an argument that names none is the same for every part. Nothing has to cross between parts.
Inputs may be any that keep to these rules, and one draw needn't show every extreme that they name: kinetic is symmetric.
All inputs are finite; a program needn't handle non-finite values.
Results may differ from a plain program's by a relative error of at most 0.0014.
Values may be sent and summed in bfloat16 or wider, within the bound.
A program may use at most 64 MiB of HBM per device.

v0:
```python
import functools

import jax
import jax.numpy as jnp
from jax import lax
from jax.experimental import pallas as pl
from jax.experimental.pallas import tpu as pltpu
from jax.sharding import PartitionSpec as P

ZL = 6
NL = 7
LINES = 19
NXN = 13
ROWS = LINES * 8
KROWS = 160
KDIM = NL * 64
PIECES = 16
STEPS = 4
F32 = jnp.float32
BF16 = jnp.bfloat16


def dot(a, b):
    return jnp.dot(a, b, preferred_element_type=F32)


def joined(first, second):
    row = lax.broadcasted_iota(jnp.int32, first.shape, 1)
    moved_second = pltpu.roll(second, 6, 1)
    moved_first = pltpu.roll(first, 2, 1)
    return (
        first + jnp.where(row == 6, moved_second, 0.0),
        second + jnp.where(row == 0, moved_first, 0.0),
    )


def wave_lines(layer):
    layer = layer.astype(F32)
    empty = jnp.zeros((LINES, 1, layer.shape[2]), F32)
    return layer[:, 0:8], jnp.concatenate([layer[:, 6:NXN], empty], axis=1)


def kernel(
    n, scale, pc, pp, center, hw, wave, kin, pot, pv, coup, out,
    Y, Vb, G, L1, L2, U, M, acc, pot6, pvx, meta, ini_s, ini_r,
    up_s, up_r, dn_s, dn_r, coef, cpl,
    meta_ss, meta_rs, set_ss, set_rs, coef_ss, coef_rs, pl_ss, pl_rs,
):
    me = lax.axis_index("dom")
    cols = wave.shape[3]

    def to(offset):
        return {"dom": lax.rem(me + offset, n)}

    def copy(src, dst, ss, rs, offset):
        return pltpu.make_async_remote_copy(
            src_ref=src, dst_ref=dst, send_sem=ss, recv_sem=rs,
            device_id=to(offset), device_id_type=pl.DeviceIdType.MESH,
        )

    barrier = pltpu.get_barrier_semaphore()
    for r in range(1, n):
        pl.semaphore_signal(barrier, inc=1, device_id=to(r), device_id_type=pl.DeviceIdType.MESH)

    first, second = wave_lines(wave[0])
    ini_s[...] = jnp.concatenate([first, second], axis=1).astype(BF16).reshape(LINES * 16, cols)
    row = lax.broadcasted_iota(jnp.int32, (PIECES, 128), 0)
    lane = lax.broadcasted_iota(jnp.int32, (PIECES, 128), 1)
    table = jnp.zeros((PIECES, 128), jnp.int32)
    for i in range(PIECES):
        table = jnp.where(row == i, jnp.where(lane < 64, pp[i], pc[i]), table)
    meta[0] = table.astype(F32)

    pl.semaphore_wait(barrier, n - 1)
    setup = [
        copy(ini_s, ini_r, set_ss.at[0], set_rs.at[0], n - 1),
        copy(pot.at[0], pot6, set_ss.at[1], set_rs.at[1], n - 1),
        copy(pv, pvx.at[0], set_ss.at[2], set_rs.at[2], n - 1),
        copy(pv, pvx.at[1], set_ss.at[3], set_rs.at[3], 1),
    ]
    for c in setup:
        c.start()
    metas = [copy(meta.at[0], meta.at[r], meta_ss.at[r], meta_rs.at[r], r) for r in range(1, n)]
    for c in metas:
        c.start()

    def place(index):
        a, b, c = index // 64, (index // 8) % 8, index % 8
        return jnp.where((b < 7) & (c < 7), a * 49 + b * 7 + c, -1)

    nodes = kin.shape[0]
    spread = (
        lax.broadcasted_iota(jnp.int32, (nodes, KDIM), 0)
        == place(lax.broadcasted_iota(jnp.int32, (1, KDIM), 1))
    ).astype(F32).astype(BF16)
    spread_t = (
        lax.broadcasted_iota(jnp.int32, (KDIM, nodes), 1)
        == place(lax.broadcasted_iota(jnp.int32, (KDIM, 1), 0))
    ).astype(F32).astype(BF16)
    full = dot(spread_t, dot(kin[...], spread).astype(BF16))
    ends = jnp.concatenate([full[0:56], full[384:440]], axis=0)
    inner = [full[64 * a : 64 * a + 56] for a in range(1, ZL)]
    L2[...] = jnp.concatenate(inner + [jnp.zeros((8, KDIM), F32)], axis=0).astype(BF16)
    own = dot(pv[...], spread)
    own_cell = meta[0][:, 64:65]
    for cell in range(6):
        L1[cell] = jnp.concatenate([jnp.where(own_cell == float(cell), own, 0.0), ends], axis=0).astype(BF16)

    inv = 1.0 / hw[0]

    def put_shift(a, layer):
        wide = jnp.broadcast_to(layer[:, None, :], (LINES, 8, NXN))
        for cx in range(2):
            pick = (
                lax.broadcasted_iota(jnp.int32, wide.shape, 2)
                == lax.broadcasted_iota(jnp.int32, wide.shape, 1) + 6 * cx
            )
            value = jnp.sum(jnp.where(pick, wide, 0.0), axis=2, keepdims=True)
            value = jnp.broadcast_to((value - center[0]) * inv, (LINES, 8, 128))
            G[cx, a] = value.reshape(ROWS, 128)

    def put_start(a, pair):
        for cx in range(2):
            flat = pair[cx].reshape(ROWS, cols)
            Y[0, cx, a] = flat
            Y[1, cx, a] = jnp.zeros((ROWS, cols), F32)
            put_operand(cx, a, flat)

    def put_operand(cx, a, flat):
        Vb[cx, a] = jnp.concatenate([flat, jnp.zeros((8, cols), F32)], axis=0).astype(BF16)

    for a in range(ZL):
        put_start(a, wave_lines(wave[a]))
        put_shift(a, pot[a])

    for c in setup + metas:
        c.wait_recv()
    arrived = ini_r[...].astype(F32).reshape(LINES, 16, cols)
    put_start(ZL, (arrived[:, 0:8], arrived[:, 8:16]))
    put_shift(ZL, pot6[...])

    values = jnp.concatenate([pv[...], pvx[0], pvx[1]], axis=0).astype(F32)
    table = jnp.concatenate([meta[0], meta[n - 1], meta[1]], axis=0)
    cells = table[:, 64:65]
    group = lax.broadcasted_iota(jnp.int32, (56, 3 * PIECES), 1)
    parts = []
    for cell in range(6):
        masked = jnp.where(cells == float(cell), values, 0.0).astype(BF16)
        base = lax.dot_general(spread_t, masked, (((1,), (1,)), ((), ())), preferred_element_type=F32)
        low, high = base[0:56], base[384:440]
        layers = []
        for a in range(NL):
            here = jnp.where(group < PIECES, base[64 * a : 64 * a + 56], 0.0)
            if a == 0:
                here = here + jnp.where(group >= 2 * PIECES, high, 0.0)
            if a == ZL:
                here = here + jnp.where((group >= PIECES) & (group < 2 * PIECES), low, 0.0)
            layers.append(here)
        parts.append(layers)
    for a in range(NL):
        pair = []
        for cx in range(2):
            c0, c1, c2 = (parts[2 * cy + cx][a] for cy in range(3))
            whole = jnp.concatenate(
                [c0[0:48], c0[48:56] + c1[0:8], c1[8:48], c1[48:56] + c2[0:8], c2[8:56]], axis=0
            )
            pair.append(whole.reshape(LINES, 8, 3 * PIECES))
        for cx, whole in enumerate(joined(*pair)):
            flat = whole.reshape(ROWS, 3 * PIECES)
            U[cx, a] = jnp.concatenate([flat, jnp.zeros((8, 3 * PIECES), F32)], axis=0).astype(BF16)

    count = coup.shape[1]
    number = lax.broadcasted_iota(jnp.int32, (1, count), 1).astype(F32)
    hot = jnp.where(table[:, 0:1] == number, 1.0, 0.0)
    every = jnp.where(meta[...].reshape(n * PIECES, 128)[:, 0:1] == number, 1.0, 0.0).astype(BF16)
    M[...] = lax.dot_general(
        hot.astype(BF16), every, (((1,), (1,)), ((), ())), preferred_element_type=F32
    ).astype(BF16)
    cpl[...] = jnp.broadcast_to(
        jnp.sum(hot * coup[...], axis=1, keepdims=True), (3 * PIECES, cols)
    )

    def add_cell(cx, cy, a, part):
        if cy == 0:
            acc[cx, a, 0:56] = part
        else:
            acc[cx, a, 48 * cy : 48 * cy + 8] += part[0:8]
            acc[cx, a, 48 * cy + 8 : 48 * cy + 56] = part[8:56]

    def both(a):
        return joined(
            acc[0, a].reshape(LINES, 8, cols), acc[1, a].reshape(LINES, 8, cols)
        )

    def step(k, last):
        cur = lax.rem(k, 2)
        other = 1 - cur
        is_first = (k == 0) if isinstance(k, int) else None
        if is_first is None:
            factor = jnp.where(k == 0, 1.0, 2.0)
            back = jnp.where(k == 0, 0.0, 1.0)
        else:
            factor = 1.0 if is_first else 2.0
            back = 0.0 if is_first else 1.0
        gain = factor * inv

        def operand(cx, cy):
            return Vb[cx, :, 48 * cy : 48 * cy + 64, :].reshape(KDIM, cols)

        total = jnp.zeros((PIECES, cols), F32)
        for cy in range(3):
            for cx in range(2):
                cell = 2 * cy + cx
                result = dot(L1[cell], operand(cx, cy))
                total = total + result[0:PIECES]
                factor_c = scale[cell]
                add_cell(cx, cy, 0, result[16:72] * factor_c)
                add_cell(cx, cy, ZL, result[72:128] * factor_c)
        coef[k, 0] = total.astype(BF16)
        coefs = [
            copy(coef.at[k, 0], coef.at[k, r], coef_ss.at[k, r], coef_rs.at[k, r], r) for r in range(1, n)
        ]
        for c in coefs:
            c.start()
        planes = []
        ends = [ZL] if last else [ZL, 0]
        for a in ends:
            pair = both(a)
            packed = jnp.concatenate(pair, axis=1).astype(BF16).reshape(LINES * 16, cols)
            if a == ZL:
                up_s[k] = packed
                c = copy(up_s.at[k], up_r.at[k], pl_ss.at[k, 0], pl_rs.at[k, 0], 1)
            else:
                dn_s[k] = packed
                c = copy(dn_s.at[k], dn_r.at[k], pl_ss.at[k, 1], pl_rs.at[k, 1], n - 1)
            c.start()
            planes.append(c)

        for cy in range(3):
            for cx in range(2):
                result = dot(L2[...], operand(cx, cy)) * scale[2 * cy + cx]
                for a in range(1, ZL):
                    add_cell(cx, cy, a, result[56 * (a - 1) : 56 * a])

        def partial(a):
            for cx, whole in enumerate(both(a)):
                shift = G[cx, a] * factor
                shift = jnp.concatenate([shift] * (cols // 128), axis=1)
                Y[other, cx, a] = (
                    whole.reshape(ROWS, cols) * gain + shift * Y[cur, cx, a] - back * Y[other, cx, a]
                )

        for a in range(ZL if last else NL):
            partial(a)

        for c in coefs:
            c.wait_recv()
        scaled = dot(M[...], coef[k].reshape(n * PIECES, cols)) * cpl[...]
        scaled = scaled.astype(BF16)

        def finish(a, extra):
            pair = []
            for cx in range(2):
                far = dot(U[cx, a], scaled)[0:ROWS]
                if extra is not None:
                    far = far + extra[cx].reshape(ROWS, cols)
                new = Y[other, cx, a] + gain * far
                if last:
                    pair.append(new.reshape(LINES, 8, cols))
                else:
                    Y[other, cx, a] = new
                    put_operand(cx, a, new)
            if last:
                out[a] = jnp.concatenate([pair[0][:, 0:7], pair[1][:, 1:7]], axis=1)

        for a in range(1, ZL):
            finish(a, None)
        for c in planes:
            c.wait_recv()
        got = up_r[k].astype(F32).reshape(LINES, 16, cols)
        finish(0, (got[:, 0:8], got[:, 8:16]))
        if not last:
            got = dn_r[k].astype(F32).reshape(LINES, 16, cols)
            finish(ZL, (got[:, 0:8], got[:, 8:16]))
        for c in coefs + planes:
            c.wait_send()

    @pl.loop(0, STEPS - 1)
    def _(k):
        step(k, False)

    step(STEPS - 1, True)
    for c in setup + metas:
        c.wait_send()


def local(n, wave, kinetic, cell_scale, potential, proj_values, piece_cell, piece_proj, coupling, center, halfwidth):
    cols = wave.shape[3]
    plane = (LINES * 16, cols)
    smem = pl.BlockSpec(memory_space=pltpu.SMEM)
    vmem = pl.BlockSpec(memory_space=pltpu.VMEM)
    dma = pltpu.SemaphoreType.DMA
    return pl.pallas_call(
        functools.partial(kernel, n),
        out_shape=jax.ShapeDtypeStruct(wave.shape, F32),
        in_specs=[smem] * 5 + [vmem] * 5,
        out_specs=vmem,
        scratch_shapes=[
            pltpu.VMEM((2, 2, NL, ROWS, cols), F32),
            pltpu.VMEM((2, NL, KROWS, cols), BF16),
            pltpu.VMEM((2, NL, ROWS, 128), F32),
            pltpu.VMEM((6, 128, KDIM), BF16),
            pltpu.VMEM((288, KDIM), BF16),
            pltpu.VMEM((2, NL, KROWS, 3 * PIECES), BF16),
            pltpu.VMEM((3 * PIECES, n * PIECES), BF16),
            pltpu.VMEM((2, NL, ROWS, cols), F32),
            pltpu.VMEM((LINES, NXN), F32),
            pltpu.VMEM((2,) + proj_values.shape, BF16),
            pltpu.VMEM((n, PIECES, 128), F32),
            pltpu.VMEM(plane, BF16),
            pltpu.VMEM(plane, BF16),
            pltpu.VMEM((STEPS,) + plane, BF16),
            pltpu.VMEM((STEPS,) + plane, BF16),
            pltpu.VMEM((STEPS - 1,) + plane, BF16),
            pltpu.VMEM((STEPS - 1,) + plane, BF16),
            pltpu.VMEM((STEPS, n, PIECES, cols), BF16),
            pltpu.VMEM((3 * PIECES, cols), F32),
            dma((n,)), dma((n,)), dma((4,)), dma((4,)),
            dma((STEPS, n)), dma((STEPS, n)), dma((STEPS, 2)), dma((STEPS, 2)),
        ],
        compiler_params=pltpu.CompilerParams(
            collective_id=0, has_side_effects=True, vmem_limit_bytes=48 * 1024 * 1024
        ),
        name="filter",
    )(
        cell_scale, piece_cell, piece_proj, center, halfwidth,
        wave, kinetic, potential, proj_values, coupling[None, :],
    )


def solution(mesh):
    in_specs = (
        P("dom", None, None, "band"), P(), P("dom"), P("dom", None, None), P("dom", None),
        P("dom"), P("dom"), P(), P(), P(),
    )
    return jax.shard_map(
        functools.partial(local, mesh.shape["dom"]), mesh=mesh, in_specs=in_specs,
        out_specs=P("dom", None, None, "band"), check_vma=False,
    )
```

profile of v0, /device:TPU:0, one launch (start us, length us, event | category | flops | bytes accessed | tf_op | source)
XLA Modules:
  0.0 49.0 jit_solution(7436126495107924508)
XLA Ops:
  1.3 0.9 %copy.11.pot = f32[6,19,13]{2,1,0:T(8,128)S(1)} copy(f32[6,19,13]{1,2,0:T(8,128)} %param.13) | data formatting | bytes 11856 | tf_op args[3]
  2.2 0.0 copy-start
  2.2 1.2 %copy-done = bf16[6,19,13,256]{3,2,1,0:T(8,128)(2,1)S(1)} copy-done((bf16[6,19,13,256]{3,2,1,0:T(8,128)(2,1)S(1)}, bf16[6,19,13,256]{3,2,1,0:T(8,128)(2,1)}, u32[]{:S(2)}) %copy-start) | copy-done | bytes 758808
  3.4 0.0 copy-start.1
  3.4 0.9 %copy-done.1 = bf16[343,343]{1,0:T(8,128)(2,1)S(1)} copy-done((bf16[343,343]{1,0:T(8,128)(2,1)S(1)}, bf16[343,343]{1,0:T(8,128)(2,1)}, u32[]{:S(2)}) %copy-start.1) | copy-done | bytes 235322
  4.4 0.0 copy-start.2
  4.4 0.7 %copy-done.2 = bf16[16,343]{1,0:T(8,128)(2,1)S(1)} copy-done((bf16[16,343]{1,0:T(8,128)(2,1)S(1)}, bf16[16,343]{1,0:T(8,128)(2,1)}, u32[]{:S(2)}) %copy-start.2) | copy-done | bytes 11000
  5.1 0.0 copy-start.3
  5.1 0.7 %copy-done.3 = f32[256]{0:T(256)S(1)} copy-done((f32[256]{0:T(256)S(1)}, f32[256]{0:T(256)}, u32[]{:S(2)}) %copy-start.3) | copy-done | bytes 1048
  5.7 0.0 copy-start.4
  5.7 0.7 %copy-done.4 = f32[6]{0:T(128)S(1)} copy-done((f32[6]{0:T(128)S(1)}, f32[6]{0:T(128)}, u32[]{:S(2)}) %copy-start.4) | copy-done | bytes 48
  6.4 0.0 copy-start.5
  6.4 0.7 %copy-done.5 = s32[16]{0:T(128)S(1)} copy-done((s32[16]{0:T(128)S(1)}, s32[16]{0:T(128)}, u32[]{:S(2)}) %copy-start.5) | copy-done | bytes 88
  7.1 0.0 copy-start.6
  7.1 0.7 %copy-done.6 = s32[16]{0:T(128)S(1)} copy-done((s32[16]{0:T(128)S(1)}, s32[16]{0:T(128)}, u32[]{:S(2)}) %copy-start.6) | copy-done | bytes 88
  7.7 40.0 %filter.1 = f32[6,19,13,256]{3,2,1,0:T(8,128)S(1)} custom-call(f32[6]{0:T(128)S(1)} %copy-done.4, s32[16]{0:T(128)S(1)} %copy-done.5, s32[16]{0:T(128)S(1)} %copy-done.6, f32[1]{0:T(128)S(6)} %copy.13.center, f32[1]{0:T(128)S(6)} %copy.14.hw, bf16[6,19,13,256]{3,2,1,0:T(8,128)(2,1)S(1)} %copy-done, bf16[343,343]{1,0:T(8,128)(2,1)S(1)} %copy-done.1, ...), custom_call_target="tpu_custom_call" | custom-call | tf_op jit(solution)/shard_map/filter/pallas_call | solution.py:303
  47.7 1.2 %copy.15 = f32[6,19,13,256]{3,2,1,0:T(8,128)} copy(f32[6,19,13,256]{3,2,1,0:T(8,128)S(1)} %filter.1) | data formatting | bytes 3035136
Async XLA Ops:
  2.2 1.2 %copy-start = (bf16[6,19,13,256]{3,2,1,0:T(8,128)(2,1)S(1)}, bf16[6,19,13,256]{3,2,1,0:T(8,128)(2,1)}, u32[]{:S(2)}) copy-start(bf16[6,19,13,256]{3,2,1,0:T(8,128)(2,1)} %wave.1) | copy-start | bytes 2276356
  3.4 1.0 %copy-start.1 = (bf16[343,343]{1,0:T(8,128)(2,1)S(1)}, bf16[343,343]{1,0:T(8,128)(2,1)}, u32[]{:S(2)}) copy-start(bf16[343,343]{1,0:T(8,128)(2,1)} %kin.1) | copy-start | bytes 705898
  4.4 0.7 %copy-start.2 = (bf16[16,343]{1,0:T(8,128)(2,1)S(1)}, bf16[16,343]{1,0:T(8,128)(2,1)}, u32[]{:S(2)}) copy-start(bf16[16,343]{1,0:T(8,128)(2,1)} %pv.1) | copy-start | bytes 32932
  5.1 0.7 %copy-start.3 = (f32[256]{0:T(256)S(1)}, f32[256]{0:T(256)}, u32[]{:S(2)}) copy-start(f32[256]{0:T(256)} %param.17) | copy-start | bytes 3076
  5.7 0.7 %copy-start.4 = (f32[6]{0:T(128)S(1)}, f32[6]{0:T(128)}, u32[]{:S(2)}) copy-start(f32[6]{0:T(128)} %scale.1) | copy-start | bytes 76
  6.4 0.7 %copy-start.5 = (s32[16]{0:T(128)S(1)}, s32[16]{0:T(128)}, u32[]{:S(2)}) copy-start(s32[16]{0:T(128)} %pc.1) | copy-start | bytes 196
  7.1 0.7 %copy-start.6 = (s32[16]{0:T(128)S(1)}, s32[16]{0:T(128)}, u32[]{:S(2)}) copy-start(s32[16]{0:T(128)} %pp.1) | copy-start | bytes 196
where the time goes:
time: 49.3 us; the launch traced here: 49 us
  Pallas kernels  40 us (81%)
  local copies, waits for them, and re-layouts  7.64 us (15%)
  between operations  1.31 us (3%)
    pallas_call x1, Pallas kernels, local(): pl.pallas_call(functools.partial(kernel, n), out_shape=jax.ShapeDtypeStru...  40 us
    unnamed x16, local copies, waits for them, and re-layouts  7.64 us

commit v1 on v0

--- a/solution.py
+++ b/solution.py
@@ -41,13 +41,23 @@
 
 
 def kernel(
-    n, scale, pc, pp, center, hw, wave, kin, pot, pv, coup, out,
+    n, scale, pc, pp, center, hw, wave_hbm, kin_hbm, pot_hbm, pv_hbm, coup, out,
+    wave, kin, pot, pv, in_sem,
     Y, Vb, G, L1, L2, U, M, acc, pot6, pvx, meta, ini_s, ini_r,
     up_s, up_r, dn_s, dn_r, coef, cpl,
     meta_ss, meta_rs, set_ss, set_rs, coef_ss, coef_rs, pl_ss, pl_rs,
 ):
     me = lax.axis_index("dom")
     cols = wave.shape[3]
+    loads = [
+        pltpu.make_async_copy(wave_hbm.at[0], wave.at[0], in_sem.at[0]),
+        pltpu.make_async_copy(pot_hbm, pot, in_sem.at[1]),
+        pltpu.make_async_copy(pv_hbm, pv, in_sem.at[2]),
+        pltpu.make_async_copy(kin_hbm, kin, in_sem.at[3]),
+        pltpu.make_async_copy(wave_hbm.at[1:ZL], wave.at[1:ZL], in_sem.at[4]),
+    ]
+    for c in loads:
+        c.start()
 
     def to(offset):
         return {"dom": lax.rem(me + offset, n)}
@@ -62,6 +72,7 @@
     for r in range(1, n):
         pl.semaphore_signal(barrier, inc=1, device_id=to(r), device_id_type=pl.DeviceIdType.MESH)
 
+    loads[0].wait()
     first, second = wave_lines(wave[0])
     ini_s[...] = jnp.concatenate([first, second], axis=1).astype(BF16).reshape(LINES * 16, cols)
     row = lax.broadcasted_iota(jnp.int32, (PIECES, 128), 0)
@@ -71,6 +82,8 @@
         table = jnp.where(row == i, jnp.where(lane < 64, pp[i], pc[i]), table)
     meta[0] = table.astype(F32)
 
+    loads[1].wait()
+    loads[2].wait()
     pl.semaphore_wait(barrier, n - 1)
     setup = [
         copy(ini_s, ini_r, set_ss.at[0], set_rs.at[0], n - 1),
@@ -88,6 +101,7 @@
         a, b, c = index // 64, (index // 8) % 8, index % 8
         return jnp.where((b < 7) & (c < 7), a * 49 + b * 7 + c, -1)
 
+    loads[3].wait()
     nodes = kin.shape[0]
     spread = (
         lax.broadcasted_iota(jnp.int32, (nodes, KDIM), 0)
@@ -109,15 +123,13 @@
     inv = 1.0 / hw[0]
 
     def put_shift(a, layer):
-        wide = jnp.broadcast_to(layer[:, None, :], (LINES, 8, NXN))
+        layer = (layer - center[0]) * inv
+        layer = jnp.concatenate([layer, jnp.zeros((3, LINES), F32)], axis=0)
+        halves = (layer[0:8], pltpu.roll(layer, 10, 0)[0:8])
         for cx in range(2):
-            pick = (
-                lax.broadcasted_iota(jnp.int32, wide.shape, 2)
-                == lax.broadcasted_iota(jnp.int32, wide.shape, 1) + 6 * cx
-            )
-            value = jnp.sum(jnp.where(pick, wide, 0.0), axis=2, keepdims=True)
-            value = jnp.broadcast_to((value - center[0]) * inv, (LINES, 8, 128))
-            G[cx, a] = value.reshape(ROWS, 128)
+            for line in range(LINES):
+                column = halves[cx][:, line : line + 1]
+                G[cx, a, 8 * line : 8 * line + 8] = jnp.broadcast_to(column, (8, 128))
 
     def put_start(a, pair):
         for cx in range(2):
@@ -129,56 +141,60 @@
     def put_operand(cx, a, flat):
         Vb[cx, a] = jnp.concatenate([flat, jnp.zeros((8, cols), F32)], axis=0).astype(BF16)
 
+    loads[4].wait()
     for a in range(ZL):
         put_start(a, wave_lines(wave[a]))
         put_shift(a, pot[a])
 
-    for c in setup + metas:
+    for c in setup[:2]:
         c.wait_recv()
     arrived = ini_r[...].astype(F32).reshape(LINES, 16, cols)
     put_start(ZL, (arrived[:, 0:8], arrived[:, 8:16]))
     put_shift(ZL, pot6[...])
 
-    values = jnp.concatenate([pv[...], pvx[0], pvx[1]], axis=0).astype(F32)
-    table = jnp.concatenate([meta[0], meta[n - 1], meta[1]], axis=0)
-    cells = table[:, 64:65]
-    group = lax.broadcasted_iota(jnp.int32, (56, 3 * PIECES), 1)
-    parts = []
-    for cell in range(6):
-        masked = jnp.where(cells == float(cell), values, 0.0).astype(BF16)
-        base = lax.dot_general(spread_t, masked, (((1,), (1,)), ((), ())), preferred_element_type=F32)
-        low, high = base[0:56], base[384:440]
-        layers = []
+    def put_projectors():
+        for c in setup[2:] + metas:
+            c.wait_recv()
+        values = jnp.concatenate([pv[...], pvx[0], pvx[1]], axis=0).astype(F32)
+        table = jnp.concatenate([meta[0], meta[n - 1], meta[1]], axis=0)
+        cells = table[:, 64:65]
+        group = lax.broadcasted_iota(jnp.int32, (56, 3 * PIECES), 1)
+        parts = []
+        for cell in range(6):
+            masked = jnp.where(cells == float(cell), values, 0.0).astype(BF16)
+            base = lax.dot_general(spread_t, masked, (((1,), (1,)), ((), ())), preferred_element_type=F32)
+            low, high = base[0:56], base[384:440]
+            layers = []
+            for a in range(NL):
+                here = jnp.where(group < PIECES, base[64 * a : 64 * a + 56], 0.0)
+                if a == 0:
+                    here = here + jnp.where(group >= 2 * PIECES, high, 0.0)
+                if a == ZL:
+                    here = here + jnp.where((group >= PIECES) & (group < 2 * PIECES), low, 0.0)
+                layers.append(here)
+            parts.append(layers)
         for a in range(NL):
-            here = jnp.where(group < PIECES, base[64 * a : 64 * a + 56], 0.0)
-            if a == 0:
-                here = here + jnp.where(group >= 2 * PIECES, high, 0.0)
-            if a == ZL:
-                here = here + jnp.where((group >= PIECES) & (group < 2 * PIECES), low, 0.0)
-            layers.append(here)
-        parts.append(layers)
-    for a in range(NL):
-        pair = []
-        for cx in range(2):
-            c0, c1, c2 = (parts[2 * cy + cx][a] for cy in range(3))
-            whole = jnp.concatenate(
-                [c0[0:48], c0[48:56] + c1[0:8], c1[8:48], c1[48:56] + c2[0:8], c2[8:56]], axis=0
-            )
-            pair.append(whole.reshape(LINES, 8, 3 * PIECES))
-        for cx, whole in enumerate(joined(*pair)):
-            flat = whole.reshape(ROWS, 3 * PIECES)
-            U[cx, a] = jnp.concatenate([flat, jnp.zeros((8, 3 * PIECES), F32)], axis=0).astype(BF16)
-
-    count = coup.shape[1]
-    number = lax.broadcasted_iota(jnp.int32, (1, count), 1).astype(F32)
-    hot = jnp.where(table[:, 0:1] == number, 1.0, 0.0)
-    every = jnp.where(meta[...].reshape(n * PIECES, 128)[:, 0:1] == number, 1.0, 0.0).astype(BF16)
-    M[...] = lax.dot_general(
-        hot.astype(BF16), every, (((1,), (1,)), ((), ())), preferred_element_type=F32
-    ).astype(BF16)
-    cpl[...] = jnp.broadcast_to(
-        jnp.sum(hot * coup[...], axis=1, keepdims=True), (3 * PIECES, cols)
-    )
+            pair = []
+            for cx in range(2):
+                c0, c1, c2 = (parts[2 * cy + cx][a] for cy in range(3))
+                whole = jnp.concatenate(
+                    [c0[0:48], c0[48:56] + c1[0:8], c1[8:48], c1[48:56] + c2[0:8], c2[8:56]], axis=0
+                )
+                pair.append(whole.reshape(LINES, 8, 3 * PIECES))
+            for cx, whole in enumerate(joined(*pair)):
+                flat = whole.reshape(ROWS, 3 * PIECES)
+                U[cx, a] = jnp.concatenate([flat, jnp.zeros((8, 3 * PIECES), F32)], axis=0).astype(BF16)
+
+        count = coup.shape[1]
+        number = lax.broadcasted_iota(jnp.int32, (1, count), 1).astype(F32)
+        hot = jnp.where(table[:, 0:1] == number, 1.0, 0.0)
+        every = jnp.where(meta[...].reshape(n * PIECES, 128)[:, 0:1] == number, 1.0, 0.0).astype(BF16)
+        M[...] = lax.dot_general(
+            hot.astype(BF16), every, (((1,), (1,)), ((), ())), preferred_element_type=F32
+        ).astype(BF16)
+        cpl[...] = jnp.broadcast_to(
+            jnp.sum(hot * coup[...], axis=1, keepdims=True), (3 * PIECES, cols)
+        )
 
     def add_cell(cx, cy, a, part):
         if cy == 0:
@@ -193,15 +209,11 @@
         )
 
     def step(k, last):
-        cur = lax.rem(k, 2)
+        cur = k % 2
         other = 1 - cur
-        is_first = (k == 0) if isinstance(k, int) else None
-        if is_first is None:
-            factor = jnp.where(k == 0, 1.0, 2.0)
-            back = jnp.where(k == 0, 0.0, 1.0)
-        else:
-            factor = 1.0 if is_first else 2.0
-            back = 0.0 if is_first else 1.0
+        starts = isinstance(k, int) and k == 0
+        factor = 1.0 if starts else 2.0
+        back = 0.0 if starts else 1.0
         gain = factor * inv
 
         def operand(cx, cy):
@@ -253,6 +265,8 @@
         for a in range(ZL if last else NL):
             partial(a)
 
+        if isinstance(k, int) and k == 0:
+            put_projectors()
         for c in coefs:
             c.wait_recv()
         scaled = dot(M[...], coef[k].reshape(n * PIECES, cols)) * cpl[...]
@@ -285,7 +299,9 @@
         for c in coefs + planes:
             c.wait_send()
 
-    @pl.loop(0, STEPS - 1)
+    step(0, False)
+
+    @pl.loop(1, STEPS - 1)
     def _(k):
         step(k, False)
 
@@ -298,14 +314,20 @@
     cols = wave.shape[3]
     plane = (LINES * 16, cols)
     smem = pl.BlockSpec(memory_space=pltpu.SMEM)
+    hbm = pl.BlockSpec(memory_space=pltpu.HBM)
     vmem = pl.BlockSpec(memory_space=pltpu.VMEM)
     dma = pltpu.SemaphoreType.DMA
     return pl.pallas_call(
         functools.partial(kernel, n),
         out_shape=jax.ShapeDtypeStruct(wave.shape, F32),
-        in_specs=[smem] * 5 + [vmem] * 5,
+        in_specs=[smem] * 5 + [hbm] * 4 + [vmem],
         out_specs=vmem,
         scratch_shapes=[
+            pltpu.VMEM(wave.shape, BF16),
+            pltpu.VMEM(kinetic.shape, BF16),
+            pltpu.VMEM((ZL, NXN, LINES), F32),
+            pltpu.VMEM(proj_values.shape, BF16),
+            dma((5,)),
             pltpu.VMEM((2, 2, NL, ROWS, cols), F32),
             pltpu.VMEM((2, NL, KROWS, cols), BF16),
             pltpu.VMEM((2, NL, ROWS, 128), F32),
@@ -314,7 +336,7 @@
             pltpu.VMEM((2, NL, KROWS, 3 * PIECES), BF16),
             pltpu.VMEM((3 * PIECES, n * PIECES), BF16),
             pltpu.VMEM((2, NL, ROWS, cols), F32),
-            pltpu.VMEM((LINES, NXN), F32),
+            pltpu.VMEM((NXN, LINES), F32),
             pltpu.VMEM((2,) + proj_values.shape, BF16),
             pltpu.VMEM((n, PIECES, 128), F32),
             pltpu.VMEM(plane, BF16),
@@ -329,12 +351,12 @@
             dma((STEPS, n)), dma((STEPS, n)), dma((STEPS, 2)), dma((STEPS, 2)),
         ],
         compiler_params=pltpu.CompilerParams(
-            collective_id=0, has_side_effects=True, vmem_limit_bytes=48 * 1024 * 1024
+            collective_id=0, has_side_effects=True, vmem_limit_bytes=64 * 1024 * 1024 - 65536
         ),
         name="filter",
     )(
         cell_scale, piece_cell, piece_proj, center, halfwidth,
-        wave, kinetic, potential, proj_values, coupling[None, :],
+        wave, kinetic, potential.transpose(0, 2, 1), proj_values, coupling[None, :],
     )
 
 

time: 49.3 us -> 42.6 us (0.86)
  local copies, waits for them, and re-layouts: 7.64 us -> 2.94 us
  Pallas kernels: 40 us -> 38.2 us
    unnamed x16 -> x1, local copies, waits for them, and re-layouts: 7.64 us -> 2.94 us
    pallas_call x1, Pallas kernels: 40 us -> 38.2 us  [local(): pl.pallas_call(functools.partial(kernel, n), out_shape=jax.ShapeDtypeStru...]
where the time goes in v1:
time: 42.6 us; the launch traced here: 42.4 us
  Pallas kernels  38.2 us (90%)
  local copies, waits for them, and re-layouts  2.94 us (7%)
  between operations  1.3 us (3%)
    pallas_call x1, Pallas kernels, local(): pl.pallas_call(functools.partial(kernel, n), out_shape=jax.ShapeDtypeStru...  38.2 us
    unnamed x1, local copies, waits for them, and re-layouts  2.94 us

profile of v1, /device:TPU:0, one launch (start us, length us, event | category | flops | bytes accessed | tf_op | source)
XLA Modules:
  0.0 42.4 jit_solution(1675121190909752748)
XLA Ops:
  1.3 38.2 %filter.1 = f32[6,19,13,256]{3,2,1,0:T(8,128)} custom-call(f32[6]{0:T(128)} %scale.1, s32[16]{0:T(128)} %pc.1, s32[16]{0:T(128)} %pp.1, f32[1]{0:T(128)S(6)} %copy.12.center, f32[1]{0:T(128)S(6)} %copy.13.hw, bf16[6,19,13,256]{3,2,1,0:T(8,128)(2,1)} %wave_hbm.1, bf16[343,343]{1,0:T(8,128)(2,1)} %kin_hbm.1, f32[6,13,19]{2,1,0:T(8,128)} %bitcast.2, ...), custom_call_target="tpu_custom_call" | custom-call | tf_op jit(solution)/shard_map/filter/pallas_call | solution.py:320
  39.5 2.9 %copy.14 = f32[6,19,13,256]{3,2,1,0:T(8,128)} copy(f32[6,19,13,256]{3,2,1,0:T(8,128)} %filter.1) | data formatting | bytes 3035136

commit v2 on v1

--- a/solution.py
+++ b/solution.py
@@ -48,6 +48,7 @@
     meta_ss, meta_rs, set_ss, set_rs, coef_ss, coef_rs, pl_ss, pl_rs,
 ):
     me = lax.axis_index("dom")
+    half, chip, core = n // 2, me // 2, me % 2
     cols = wave.shape[3]
     loads = [
         pltpu.make_async_copy(wave_hbm.at[0], wave.at[0], in_sem.at[0]),
@@ -188,7 +189,9 @@
         count = coup.shape[1]
         number = lax.broadcasted_iota(jnp.int32, (1, count), 1).astype(F32)
         hot = jnp.where(table[:, 0:1] == number, 1.0, 0.0)
-        every = jnp.where(meta[...].reshape(n * PIECES, 128)[:, 0:1] == number, 1.0, 0.0).astype(BF16)
+        ordered = [meta[lax.rem(me - 2 * c - p + n, n)] for p in range(2) for c in range(half)]
+        ordered = jnp.concatenate(ordered, axis=0)
+        every = jnp.where(ordered[:, 0:1] == number, 1.0, 0.0).astype(BF16)
         M[...] = lax.dot_general(
             hot.astype(BF16), every, (((1,), (1,)), ((), ())), preferred_element_type=F32
         ).astype(BF16)
@@ -228,9 +231,10 @@
                 factor_c = scale[cell]
                 add_cell(cx, cy, 0, result[16:72] * factor_c)
                 add_cell(cx, cy, ZL, result[72:128] * factor_c)
-        coef[k, 0] = total.astype(BF16)
+        coef[k, core, chip] = total.astype(BF16)
         coefs = [
-            copy(coef.at[k, 0], coef.at[k, r], coef_ss.at[k, r], coef_rs.at[k, r], r) for r in range(1, n)
+            copy(coef.at[k, core, chip], coef.at[k, core, chip], coef_ss.at[k, r], coef_rs.at[k, r], 2 * r)
+            for r in range(1, half)
         ]
         for c in coefs:
             c.start()
@@ -254,6 +258,11 @@
                 for a in range(1, ZL):
                     add_cell(cx, cy, a, result[56 * (a - 1) : 56 * a])
 
+        for c in coefs:
+            c.wait_recv()
+        handed = copy(coef.at[k, core], coef.at[k, core], coef_ss.at[k, 0], coef_rs.at[k, 0], 1 + core * (n - 2))
+        handed.start()
+
         def partial(a):
             for cx, whole in enumerate(both(a)):
                 shift = G[cx, a] * factor
@@ -267,8 +276,7 @@
 
         if isinstance(k, int) and k == 0:
             put_projectors()
-        for c in coefs:
-            c.wait_recv()
+        handed.wait_recv()
         scaled = dot(M[...], coef[k].reshape(n * PIECES, cols)) * cpl[...]
         scaled = scaled.astype(BF16)
 
@@ -296,7 +304,7 @@
         if not last:
             got = dn_r[k].astype(F32).reshape(LINES, 16, cols)
             finish(ZL, (got[:, 0:8], got[:, 8:16]))
-        for c in coefs + planes:
+        for c in coefs + [handed] + planes:
             c.wait_send()
 
     step(0, False)
@@ -345,10 +353,10 @@
             pltpu.VMEM((STEPS,) + plane, BF16),
             pltpu.VMEM((STEPS - 1,) + plane, BF16),
             pltpu.VMEM((STEPS - 1,) + plane, BF16),
-            pltpu.VMEM((STEPS, n, PIECES, cols), BF16),
+            pltpu.VMEM((STEPS, 2, n // 2, PIECES, cols), BF16),
             pltpu.VMEM((3 * PIECES, cols), F32),
             dma((n,)), dma((n,)), dma((4,)), dma((4,)),
-            dma((STEPS, n)), dma((STEPS, n)), dma((STEPS, 2)), dma((STEPS, 2)),
+            dma((STEPS, n // 2)), dma((STEPS, n // 2)), dma((STEPS, 2)), dma((STEPS, 2)),
         ],
         compiler_params=pltpu.CompilerParams(
             collective_id=0, has_side_effects=True, vmem_limit_bytes=64 * 1024 * 1024 - 65536

time: 42.6 us -> 41.7 us (0.979)
  Pallas kernels: 38.2 us -> 37.3 us
    pallas_call x1, Pallas kernels: 38.2 us -> 37.3 us  [local(): pl.pallas_call(functools.partial(kernel, n), out_shape=jax.ShapeDtypeStru...]
where the time goes in v2:
time: 41.7 us; the launch traced here: 41.5 us
  Pallas kernels  37.3 us (89%)
  local copies, waits for them, and re-layouts  2.94 us (7%)
  between operations  1.3 us (3%)
    pallas_call x1, Pallas kernels, local(): pl.pallas_call(functools.partial(kernel, n), out_shape=jax.ShapeDtypeStru...  37.3 us
    unnamed x1, local copies, waits for them, and re-layouts  2.94 us

profile of v2, /device:TPU:0, one launch (start us, length us, event | category | flops | bytes accessed | tf_op | source)
XLA Modules:
  0.0 41.5 jit_solution(6876129072457066169)
XLA Ops:
  1.3 37.3 %filter.1 = f32[6,19,13,256]{3,2,1,0:T(8,128)} custom-call(f32[6]{0:T(128)} %scale.1, s32[16]{0:T(128)} %pc.1, s32[16]{0:T(128)} %pp.1, f32[1]{0:T(128)S(6)} %copy.12.center, f32[1]{0:T(128)S(6)} %copy.13.hw, bf16[6,19,13,256]{3,2,1,0:T(8,128)(2,1)} %wave_hbm.1, bf16[343,343]{1,0:T(8,128)(2,1)} %kin_hbm.1, f32[6,13,19]{2,1,0:T(8,128)} %bitcast.2, ...), custom_call_target="tpu_custom_call" | custom-call | tf_op jit(solution)/shard_map/filter/pallas_call | solution.py:328
  38.6 2.9 %copy.14 = f32[6,19,13,256]{3,2,1,0:T(8,128)} copy(f32[6,19,13,256]{3,2,1,0:T(8,128)} %filter.1) | data formatting | bytes 3035136

commit v3 on v2

--- a/solution.py
+++ b/solution.py
@@ -38,6 +38,35 @@
     layer = layer.astype(F32)
     empty = jnp.zeros((LINES, 1, layer.shape[2]), F32)
     return layer[:, 0:8], jnp.concatenate([layer[:, 6:NXN], empty], axis=1)
+
+
+SPARE = (7, 8, 15)
+
+
+def pack(pair):
+    whole = jnp.concatenate(pair, axis=1)
+    cols = whole.shape[2]
+    packed = whole[0:16]
+    row = lax.broadcasted_iota(jnp.int32, packed.shape, 1)
+    for i, spare in enumerate(SPARE):
+        line = whole[16 + i]
+        nodes = jnp.concatenate([line[0:7], line[9:15], jnp.zeros((3, cols), F32)], axis=0)
+        packed = jnp.where(row == spare, jnp.broadcast_to(nodes[:, None, :], packed.shape), packed)
+    return packed.astype(BF16).reshape(256, cols)
+
+
+def unpack(packed):
+    cols = packed.shape[1]
+    whole = packed.astype(F32).reshape(16, 16, cols)
+    first, second = whole[:, 0:8], whole[:, 8:16]
+    row = lax.broadcasted_iota(jnp.int32, first.shape, 1)
+    firsts = [first]
+    seconds = [jnp.where(row == 0, pltpu.roll(first, 2, 1), second)]
+    for spare in SPARE:
+        nodes = whole[:, spare]
+        firsts.append(nodes[0:8][None])
+        seconds.append(jnp.concatenate([nodes[6:13], jnp.zeros((1, cols), F32)], axis=0)[None])
+    return jnp.concatenate(firsts, axis=0), jnp.concatenate(seconds, axis=0)
 
 
 def kernel(
@@ -74,8 +103,7 @@
         pl.semaphore_signal(barrier, inc=1, device_id=to(r), device_id_type=pl.DeviceIdType.MESH)
 
     loads[0].wait()
-    first, second = wave_lines(wave[0])
-    ini_s[...] = jnp.concatenate([first, second], axis=1).astype(BF16).reshape(LINES * 16, cols)
+    ini_s[...] = pack(wave_lines(wave[0]))
     row = lax.broadcasted_iota(jnp.int32, (PIECES, 128), 0)
     lane = lax.broadcasted_iota(jnp.int32, (PIECES, 128), 1)
     table = jnp.zeros((PIECES, 128), jnp.int32)
@@ -149,8 +177,7 @@
 
     for c in setup[:2]:
         c.wait_recv()
-    arrived = ini_r[...].astype(F32).reshape(LINES, 16, cols)
-    put_start(ZL, (arrived[:, 0:8], arrived[:, 8:16]))
+    put_start(ZL, unpack(ini_r[...]))
     put_shift(ZL, pot6[...])
 
     def put_projectors():
@@ -242,7 +269,7 @@
         ends = [ZL] if last else [ZL, 0]
         for a in ends:
             pair = both(a)
-            packed = jnp.concatenate(pair, axis=1).astype(BF16).reshape(LINES * 16, cols)
+            packed = pack(pair)
             if a == ZL:
                 up_s[k] = packed
                 c = copy(up_s.at[k], up_r.at[k], pl_ss.at[k, 0], pl_rs.at[k, 0], 1)
@@ -299,11 +326,9 @@
             finish(a, None)
         for c in planes:
             c.wait_recv()
-        got = up_r[k].astype(F32).reshape(LINES, 16, cols)
-        finish(0, (got[:, 0:8], got[:, 8:16]))
+        finish(0, unpack(up_r[k]))
         if not last:
-            got = dn_r[k].astype(F32).reshape(LINES, 16, cols)
-            finish(ZL, (got[:, 0:8], got[:, 8:16]))
+            finish(ZL, unpack(dn_r[k]))
         for c in coefs + [handed] + planes:
             c.wait_send()
 
@@ -320,7 +345,7 @@
 
 def local(n, wave, kinetic, cell_scale, potential, proj_values, piece_cell, piece_proj, coupling, center, halfwidth):
     cols = wave.shape[3]
-    plane = (LINES * 16, cols)
+    plane = (256, cols)
     smem = pl.BlockSpec(memory_space=pltpu.SMEM)
     hbm = pl.BlockSpec(memory_space=pltpu.HBM)
     vmem = pl.BlockSpec(memory_space=pltpu.VMEM)

time: 41.7 us -> 40.6 us (0.974)
  Pallas kernels: 37.3 us -> 36.2 us
    pallas_call x1, Pallas kernels: 37.3 us -> 36.2 us  [local(): pl.pallas_call(functools.partial(kernel, n), out_shape=jax.ShapeDtypeStru...]
where the time goes in v3:
time: 40.6 us; the launch traced here: 40.4 us
  Pallas kernels  36.2 us (89%)
  local copies, waits for them, and re-layouts  2.94 us (7%)
  between operations  1.3 us (3%)
    pallas_call x1, Pallas kernels, local(): pl.pallas_call(functools.partial(kernel, n), out_shape=jax.ShapeDtypeStru...  36.2 us
    unnamed x1, local copies, waits for them, and re-layouts  2.94 us

profile of v3, /device:TPU:0, one launch (start us, length us, event | category | flops | bytes accessed | tf_op | source)
XLA Modules:
  0.0 40.4 jit_solution(11781229364184923326)
XLA Ops:
  1.3 36.2 %filter.1 = f32[6,19,13,256]{3,2,1,0:T(8,128)} custom-call(f32[6]{0:T(128)} %scale.1, s32[16]{0:T(128)} %pc.1, s32[16]{0:T(128)} %pp.1, f32[1]{0:T(128)S(6)} %copy.12.center, f32[1]{0:T(128)S(6)} %copy.13.hw, bf16[6,19,13,256]{3,2,1,0:T(8,128)(2,1)} %wave_hbm.1, bf16[343,343]{1,0:T(8,128)(2,1)} %kin_hbm.1, f32[6,13,19]{2,1,0:T(8,128)} %bitcast.2, ...), custom_call_target="tpu_custom_call" | custom-call | tf_op jit(solution)/shard_map/filter/pallas_call | solution.py:353
  37.5 2.9 %copy.14 = f32[6,19,13,256]{3,2,1,0:T(8,128)} copy(f32[6,19,13,256]{3,2,1,0:T(8,128)} %filter.1) | data formatting | bytes 3035136
